TPU v7x, 32 devices: a whole 2x2x4 slice. The times are simulated.
32 devices in a mesh: groups: 1, expert: 16 (over z, y, x), hidden: 2 (over core).
Axes of the slice: x: 2, y: 2, z: 4, core: 2. Of those that a mesh axis runs over, the one named last changes fastest.
Arguments:
- tokens: bfloat16 [2048, 2048], P(('groups', 'expert')), may hold values from -6 to 6
- expert_ids: int32 [2048, 8], P(('groups', 'expert')), may hold values from 0 to 15, all different within a row; in each aligned block of 128 rows (0 to 127, 128 to 255, ...) at most 80 rows name the same one
- route_weights: float32 [2048, 8], P(('groups', 'expert')), may hold values from 0.05 to 1
- cotangent: bfloat16 [2048, 2048], P(('groups', 'expert')), may hold values from -6 to 6
- w_gate_up: bfloat16 [16, 2, 2048, 768], P('expert', None, None, 'hidden'), may hold values from -0.125 to 0.125
- w_down: bfloat16 [16, 768, 2048], P('expert', 'hidden'), may hold values from -0.21875 to 0.21875
Outputs:
- mixed: bfloat16 [2048, 2048], P(('groups', 'expert'))
- grad_tokens: bfloat16 [2048, 2048], P(('groups', 'expert'))
- grad_route: float32 [2048, 8], P(('groups', 'expert'))
- grad_down: bfloat16 [16, 768, 2048], P(('groups', 'expert'), 'hidden')
Inputs may be any that keep to these rules, and one draw needn't show every extreme that they name: `expert_ids`: each token names 8 different experts; the 128 rows of one index of expert name any one expert at most 80 times.
All inputs are finite; a program needn't handle non-finite values.
Results may differ from a plain program's by a relative error of at most 0.013.
Values may be sent and summed in bfloat16 or wider, within the bound.
A program may use at most 128 MiB of HBM per device.

v0:
```python
import jax
import jax.numpy as jnp
from jax import lax
from jax.sharding import PartitionSpec as P


def shards(tokens, expert_ids, route_weights, cotangent, w_gate_up, w_down):
    tok_dev = expert_ids.shape[0]
    chosen = expert_ids.shape[1]
    features = tokens.shape[1]
    owners = lax.axis_size("expert")
    halves = lax.axis_size("hidden")
    per_owner = min(tok_dev, max(2, tok_dev * chosen * 5 // (4 * owners)))
    share = per_owner // halves
    assigned = tok_dev * chosen
    all_slots = owners * per_owner
    flat_ids = expert_ids.reshape(assigned)
    onehot = (flat_ids[:, None] == jnp.arange(owners, dtype=jnp.int32)[None, :]).astype(jnp.int32)
    before = jnp.cumsum(onehot, 0) - onehot
    rank_within = jnp.sum(before * onehot, 1)
    slot_of = flat_ids * per_owner + rank_within
    select = (slot_of[None, :] == jnp.arange(all_slots, dtype=jnp.int32)[:, None]).astype(
        jnp.bfloat16
    )
    by_token = jnp.sum(select.reshape(all_slots, tok_dev, chosen), 2)
    send_rows = jnp.dot(by_token, tokens, preferred_element_type=jnp.float32).astype(jnp.bfloat16)
    scaled = (route_weights[:, :, None] * cotangent.astype(jnp.float32)[:, None, :]).astype(
        jnp.bfloat16
    )
    send_grad = jnp.dot(
        select, scaled.reshape(assigned, features), preferred_element_type=jnp.float32
    ).astype(jnp.bfloat16)
    send_rows = send_rows.reshape(owners, per_owner, features)
    send_grad = send_grad.reshape(owners, per_owner, features)
    mine = lax.axis_index("hidden")
    part_rows = lax.dynamic_slice_in_dim(send_rows, mine * share, share, 1)
    part_grad = lax.dynamic_slice_in_dim(send_grad, mine * share, share, 1)
    got_rows, got_grad = (
        lax.all_to_all(part_rows, "expert", split_axis=0, concat_axis=0, tiled=True),
        lax.all_to_all(part_grad, "expert", split_axis=0, concat_axis=0, tiled=True),
    )
    got_rows, got_grad = (
        lax.all_gather(got_rows[None], "hidden", axis=0, tiled=True),
        lax.all_gather(got_grad[None], "hidden", axis=0, tiled=True),
    )
    x_rows = got_rows.reshape(all_slots, features)
    d_rows = got_grad.reshape(all_slots, features)
    weights_gu = w_gate_up[0]
    down_mat = w_down[0]
    gate_up = jnp.einsum("rd,jdf->jrf", x_rows, weights_gu, preferred_element_type=jnp.float32)
    gate_val = gate_up[0]
    up_val = gate_up[1]
    sigma = jax.nn.sigmoid(gate_val)
    hidden_act = (gate_val * sigma * up_val).astype(jnp.bfloat16)
    grad_hidden = jnp.einsum("rd,fd->rf", d_rows, down_mat, preferred_element_type=jnp.float32)
    grad_gate = grad_hidden * up_val * sigma * (1.0 + gate_val * (1.0 - sigma))
    grad_up = grad_hidden * gate_val * sigma
    stacked = jnp.stack([grad_gate, grad_up]).astype(jnp.bfloat16)
    grad_down = jnp.einsum(
        "rf,rd->fd", hidden_act, d_rows, preferred_element_type=jnp.float32
    ).astype(jnp.bfloat16)[None]
    piece = hidden_act
    own_out = lax.psum_scatter(
        jnp.dot(piece, down_mat, preferred_element_type=jnp.float32).astype(jnp.bfloat16),
        "hidden",
        scatter_dimension=0,
        tiled=True,
    )
    piece = stacked
    own_grad = lax.psum_scatter(
        jnp.einsum("jrf,jdf->rd", piece, weights_gu, preferred_element_type=jnp.float32).astype(
            jnp.bfloat16
        ),
        "hidden",
        scatter_dimension=0,
        tiled=True,
    )
    out_slots, grad_slots = (
        lax.all_to_all(
            own_out.reshape(owners, share, features),
            "expert",
            split_axis=0,
            concat_axis=0,
            tiled=True,
        ),
        lax.all_to_all(
            own_grad.reshape(owners, share, features),
            "expert",
            split_axis=0,
            concat_axis=0,
            tiled=True,
        ),
    )
    out_slots = out_slots.reshape(owners * share, features)
    grad_slots = grad_slots.reshape(owners * share, features)
    my_select = lax.dynamic_slice_in_dim(
        select.reshape(owners, per_owner, assigned), mine * share, share, 1
    ).reshape(owners * share, assigned)
    out_each = jnp.einsum(
        "sa,sd->ad", my_select, out_slots, preferred_element_type=jnp.float32
    ).reshape(tok_dev, chosen, features)
    grad_each = jnp.einsum(
        "sa,sd->ad", my_select, grad_slots, preferred_element_type=jnp.float32
    ).reshape(tok_dev, chosen, features)
    mixed_part = jnp.sum(out_each * route_weights[:, :, None], 1)
    route_part = jnp.sum(out_each * cotangent.astype(jnp.float32)[:, None, :], 2)
    token_part = jnp.sum(grad_each, 1)
    mixed_sum, token_grad_sum, grad_route = (
        lax.psum(mixed_part.astype(jnp.bfloat16), "hidden").astype(jnp.float32),
        lax.psum(token_part.astype(jnp.bfloat16), "hidden").astype(jnp.float32),
        lax.psum(route_part.astype(jnp.bfloat16), "hidden").astype(jnp.float32),
    )
    mixed = mixed_sum.astype(jnp.bfloat16)
    grad_tokens = token_grad_sum.astype(jnp.bfloat16)
    return (mixed, grad_tokens, grad_route, grad_down)


def solution(mesh):
    placed = (
        P(("groups", "expert"), None),
        P(("groups", "expert"), None),
        P(("groups", "expert"), None),
        P(("groups", "expert"), None),
        P("expert", None, None, "hidden"),
        P("expert", "hidden", None),
    )
    return jax.shard_map(
        shards,
        mesh=mesh,
        in_specs=placed,
        out_specs=(
            P(("groups", "expert"), None),
            P(("groups", "expert"), None),
            P(("groups", "expert"), None),
            P(("groups", "expert"), "hidden", None),
        ),
        check_vma=False,
    )
```

profile of v0, /device:TPU:9, one launch (start us, length us, event | category | flops | bytes accessed | tf_op | source)
XLA Modules:
  0.0 372.9 jit_solution(9738233198790797999)
XLA Ops:
  8.3 4.5 %reduce-window.6 = s32[16,8,128]{2,1,0:T(8,128)S(1)} reduce-window(s32[16,8,128]{2,1,0:T(8,128)S(1)} %fusion.35, s32[]{:T(128)} %constant.8.clone.1), window={size=1x1x128 pad=0_0x0_0x127_0}, to_apply=%region_0.0 | reduce-window | flops 2080768 | bytes 131076 | tf_op jit(solution)/shard_map/reduce-window
  14.1 6.7 %fusion.7 = bf16[1280,128]{1,0:T(8,128)(2,1)S(1)} fusion(s32[128,8]{0,1:T(8,128)S(1)} %multiply_add_fusion.1), kind=kLoop, calls=%fused_computation.17 | loop fusion | flops 3768320 | bytes 331776 | tf_op jit(solution)/shard_map/reduce_sum | solution.py:25
  20.8 2.6 convolution_convert_fusion.2
  25.1 6.8 %all-to-all-start = ((bf16[16,40,2048]{2,1,0:T(8,128)(2,1)}), bf16[16,40,2048]{2,1,0:T(8,128)(2,1)}, u32[]{:S(2)}, u32[]{:S(2)}) async-start(bf16[16,40,2048]{2,1,0:T(8,128)(2,1)} %constant_dynamic-slice_fusion), calls=%async_computation | async-start | bytes 5242880 | tf_op jit(solution)/shard_map/all_to_all | solution.py:39
  34.3 54.1 %all-to-all-done = bf16[16,40,2048]{2,1,0:T(8,128)(2,1)} async-done(((bf16[16,40,2048]{2,1,0:T(8,128)(2,1)}), bf16[16,40,2048]{2,1,0:T(8,128)(2,1)}, u32[]{:S(2)}, u32[]{:S(2)}) %all-to-all-start) | async-done | bytes 2621472 | tf_op jit(solution)/shard_map/all_to_all | solution.py:39
  88.4 7.0 %convolution_convert_fusion = bf16[1280,2048]{1,0:T(8,128)(2,1)S(1)} fusion(f32[128,2048]{1,0:T(8,128)} %convert_element_type.68, f32[1024]{0:T(1024)S(1)} %mul.93, s32[1024]{0:T(1024)S(1)} %multiply_add_fusion.2), kind=kOutput, calls=%fused_computation.5 | convolution fusion | flops 5376835584 | bytes 6299648 | tf_op jit(solution)/shard_map/dot_general | solution.py:30
  95.8 65.7 %all_to_all.20 = bf16[16,40,2048]{2,1,0:T(8,128)(2,1)} all-to-all(bf16[16,40,2048]{2,1,0:T(8,128)(2,1)S(1)} %constant_dynamic-slice_fusion.2), channel_id=1, replica_groups=mesh['groups'=1,'expert'=16,'hidden'=2] {'expert'}, dimensions={0} | all-to-all | bytes 5242880 | tf_op jit(solution)/shard_map/all_to_all | solution.py:40
  161.7 8.7 %convolution_bitcast_fusion = f32[2,1280,384]{2,1,0:T(8,128)} fusion(bf16[1280,2048,1]{1,0,2:T(8,128)(2,1)} %bitcast.123, bf16[1,2,2048,384]{3,2,1,0:T(8,128)(2,1)S(1)} %copy-done), kind=kOutput, calls=%fused_computation.13 | convolution fusion | flops 4026531840 | bytes 12320768 | tf_op jit(solution)/shard_map/rd,jdf->jrf/dot_general | solution.py:50
  170.5 7.2 %all-gather.7.cloned.1.call-done = bf16[32,40,2048]{2,1,0:T(8,128)(2,1)} async-done(((bf16[16,40,2048]{2,1,0:T(8,128)(2,1)}), bf16[32,40,2048]{2,1,0:T(8,128)(2,1)}) %all-gather.7.cloned.1.call-update) | async-done | bytes 5242896 | tf_op jit(solution)/shard_map/all_gather | solution.py:44
  177.7 7.5 %fusion.31 = (bf16[1,1280,384]{2,1,0:T(8,128)(2,1)S(1)}, bf16[1,1280,384]{2,1,0:T(8,128)(2,1)S(1)}) fusion(f32[2,1280,384]{2,1,0:T(8,128)} %convolution_bitcast_fusion, bf16[1280,2048]{1,0:T(8,128)(2,1)} %bitcast.121, bf16[1,384,2048]{2,1,0:T(8,128)(2,1)} %param.11), kind=kOutput, calls=%fused_computation.48 | convolution fusion | flops 2019655680 | bytes 12713984 | tf_op jit(solution)/shard_map/rd,fd->rf/dot_general | solution.py:55
  185.2 6.1 %bitcast_convert_fusion = bf16[1280,2048]{1,0:T(8,128)(2,1)} fusion(bf16[1,2,2048,384]{3,2,1,0:T(8,128)(2,1)S(1)} %copy-done, bf16[1,1280,384]{2,1,0:T(8,128)(2,1)S(1)} %get-tuple-element.9, bf16[1,1280,384]{2,1,0:T(8,128)(2,1)S(1)} %get-tuple-element.8), kind=kOutput, calls=%fused_computation | convolution fusion | flops 4030136320 | bytes 10354688 | tf_op jit(solution)/shard_map/jrf,jdf->rd/dot_general | solution.py:71
  191.4 2.8 multiply_convert_fusion
  194.2 4.6 %convolution_convert_fusion.1 = bf16[1280,2048]{1,0:T(8,128)(2,1)} fusion(bf16[1,384,2048]{2,1,0:T(8,128)(2,1)S(1)} %copy-done.4, bf16[1,1280,384]{2,1,0:T(8,128)(2,1)S(1)} %multiply_convert_fusion), kind=kOutput, calls=%fused_computation.6 | convolution fusion | flops 2015887360 | bytes 7798784 | tf_op jit(solution)/shard_map/dot_general | solution.py:64
  198.8 7.0 %reduce-scatter.5.cloned.1.call-done = bf16[640,2048]{1,0:T(8,128)(2,1)} async-done(((bf16[1280,2048]{1,0:T(8,128)(2,1)}), bf16[640,2048]{1,0:T(8,128)(2,1)}) %reduce-scatter.5.cloned.1.call-update) | async-done | bytes 2621456 | tf_op jit(solution)/shard_map/reduce_scatter | solution.py:70
  205.8 6.4 %all-to-all-start.3 = ((bf16[16,40,2048]{2,1,0:T(8,128)(2,1)}), bf16[16,40,2048]{2,1,0:T(8,128)(2,1)S(1)}, u32[]{:S(2)}, u32[]{:S(2)}) async-start(bf16[16,40,2048]{2,1,0:T(8,128)(2,1)} %bitcast.113), calls=%async_computation.5 | async-start | bytes 5242880 | tf_op jit(solution)/shard_map/all_to_all | solution.py:86
  212.3 10.3 %reduce-scatter.3.cloned.1.call-done = bf16[640,2048]{1,0:T(8,128)(2,1)} async-done(((bf16[1280,2048]{1,0:T(8,128)(2,1)}), bf16[640,2048]{1,0:T(8,128)(2,1)}) %reduce-scatter.3.cloned.1.call-update) | async-done | bytes 2621456 | tf_op jit(solution)/shard_map/reduce_scatter | solution.py:63
  222.6 46.5 %all-to-all-done.3 = bf16[16,40,2048]{2,1,0:T(8,128)(2,1)S(1)} async-done(((bf16[16,40,2048]{2,1,0:T(8,128)(2,1)}), bf16[16,40,2048]{2,1,0:T(8,128)(2,1)S(1)}, u32[]{:S(2)}, u32[]{:S(2)}) %all-to-all-start.3) | async-done | bytes 2621472 | tf_op jit(solution)/shard_map/all_to_all | solution.py:86
  269.1 7.3 %all-to-all-start.1 = ((bf16[16,40,2048]{2,1,0:T(8,128)(2,1)}), bf16[16,40,2048]{2,1,0:T(8,128)(2,1)}, u32[]{:S(2)}, u32[]{:S(2)}) async-start(bf16[16,40,2048]{2,1,0:T(8,128)(2,1)} %bitcast.112), calls=%async_computation.2 | async-start | bytes 5242880 | tf_op jit(solution)/shard_map/all_to_all | solution.py:79
  280.5 5.6 %convolution_reduce_fusion = bf16[128,2048]{1,0:T(8,128)(2,1)} fusion(bf16[640,2048,1]{1,0,2:T(8,128)(2,1)S(1)} %bitcast.114, pred[128,8,640]{2,1,0:T(8,128)(4,1)} %bitcast.117), kind=kOutput, calls=%fused_computation.20 | convolution fusion | flops 2686189568 | bytes 3801088 | tf_op jit(solution)/shard_map/sa,sd->ad/dot_general | solution.py:102
  286.1 46.9 %all-to-all-done.1 = bf16[16,40,2048]{2,1,0:T(8,128)(2,1)} async-done(((bf16[16,40,2048]{2,1,0:T(8,128)(2,1)}), bf16[16,40,2048]{2,1,0:T(8,128)(2,1)}, u32[]{:S(2)}, u32[]{:S(2)}) %all-to-all-start.1) | async-done | bytes 2621472 | tf_op jit(solution)/shard_map/all_to_all | solution.py:79
  333.0 6.9 %multiply_reduce_fusion = (bf16[128,8]{0,1:T(8,128)(2,1)S(1)}, bf16[128,2048]{1,0:T(8,128)(2,1)}) fusion(f32[128,2048]{1,0:T(8,128)} %convert_element_type.68, f32[128,8]{0,1:T(8,128)S(1)} %copy-done.3, bf16[640,2048,1]{1,0,2:T(8,128)(2,1)} %bitcast.14, pred[128,8,640]{2,1,0:T(8,128)(4,1)} %bitcast.118), kind=kOutput, calls=%fused_computation.3 | convolution fusion | flops 2692480000 | bytes 4855808 | tf_op jit(solution)/shard_map/sa,sd->ad/dot_general | solution.py:99
  339.9 6.3 %fusion.9 = bf16[1,384,2048]{2,1,0:T(8,128)(2,1)} fusion(bf16[1280,2048]{1,0:T(8,128)(2,1)} %bitcast.122, bf16[1,1280,384]{2,1,0:T(8,128)(2,1)} %copy-done.2), kind=kOutput, calls=%fused_computation.19 | convolution fusion | flops 2014052352 | bytes 7798784 | tf_op jit(solution)/shard_map/rf,rd->fd/dot_general | solution.py:59
  346.3 4.6 %psum.23 = bf16[128,8]{0,1:T(8,128)(2,1)S(1)} all-reduce(bf16[128,8]{0,1:T(8,128)(2,1)S(1)} %get-tuple-element.4), channel_id=1, replica_groups=mesh['groups'=1,'expert'=16,'hidden'=2] {'hidden'}, use_global_device_ids=true, to_apply=%region_11.12 | all-reduce | flops 1024 | bytes 4096 | tf_op jit(solution)/shard_map/psum | solution.py:111
  351.5 11.1 %all-reduce.3.cloned.1.call-done = (bf16[128,2048]{1,0:T(8,128)(2,1)}, bf16[128,2048]{1,0:T(8,128)(2,1)}) async-done(((bf16[128,2048]{1,0:T(8,128)(2,1)}, bf16[128,2048]{1,0:T(8,128)(2,1)}), (bf16[128,2048]{1,0:T(8,128)(2,1)}, bf16[128,2048]{1,0:T(8,128)(2,1)})) %all-reduce.3.cloned.1.call-update) | async-done | bytes 1048592 | tf_op jit(solution)/shard_map/psum | solution.py:109
  (48 shorter events, 15.7 us)
Async XLA Ops:
  7.2 154.6 %copy-start = (bf16[1,2,2048,384]{3,2,1,0:T(8,128)(2,1)S(1)}, bf16[1,2,2048,384]{3,2,1,0:T(8,128)(2,1)}, u32[]{:S(2)}) copy-start(bf16[1,2,2048,384]{3,2,1,0:T(8,128)(2,1)} %param.10) | copy-start | bytes 9437188
  25.1 6.8 %copy-start.3 = (f32[128,8]{0,1:T(8,128)S(1)}, f32[128,8]{0,1:T(8,128)}, u32[]{:S(2)}) copy-start(f32[128,8]{0,1:T(8,128)} %param.8) | copy-start | bytes 12292
  25.1 63.2 %all-to-all-start = ((bf16[16,40,2048]{2,1,0:T(8,128)(2,1)}), bf16[16,40,2048]{2,1,0:T(8,128)(2,1)}, u32[]{:S(2)}, u32[]{:S(2)}) async-start(bf16[16,40,2048]{2,1,0:T(8,128)(2,1)} %constant_dynamic-slice_fusion), calls=%async_computation | async-start | bytes 5242880 | tf_op jit(solution)/shard_map/all_to_all | solution.py:39
  31.9 129.8 %all-gather.5.cloned.1.call-start = ((), (), s32[]{:S(2)}) async-start(), calls=%async_computation.8 | async-start | bytes 7864320 | tf_op jit(solution)/shard_map/all_gather | solution.py:43
  88.4 89.3 %all-gather.7.cloned.1.call-start = ((), (), s32[]{:S(2)}) async-start(), calls=%async_computation.9 | async-start | bytes 7864320 | tf_op jit(solution)/shard_map/all_gather | solution.py:44
  161.5 44.4 %reduce-scatter.5.cloned.1.call-start = ((), (), s32[]{:S(2)}) async-start(), calls=%async_computation.7 | async-start | bytes 7864320 | tf_op jit(solution)/shard_map/reduce_scatter | solution.py:70
  191.3 2.9 copy-start.4
  191.3 31.3 %reduce-scatter.3.cloned.1.call-start = ((), (), s32[]{:S(2)}) async-start(), calls=%async_computation.6 | async-start | bytes 7864320 | tf_op jit(solution)/shard_map/reduce_scatter | solution.py:63
  194.2 4.6 %copy-start.2 = (bf16[1,1280,384]{2,1,0:T(8,128)(2,1)}, bf16[1,1280,384]{2,1,0:T(8,128)(2,1)S(1)}, u32[]{:S(2)}) copy-start(bf16[1,1280,384]{2,1,0:T(8,128)(2,1)S(1)} %multiply_convert_fusion) | copy-start | bytes 2949124
  205.8 63.2 %all-to-all-start.3 = ((bf16[16,40,2048]{2,1,0:T(8,128)(2,1)}), bf16[16,40,2048]{2,1,0:T(8,128)(2,1)S(1)}, u32[]{:S(2)}, u32[]{:S(2)}) async-start(bf16[16,40,2048]{2,1,0:T(8,128)(2,1)} %bitcast.113), calls=%async_computation.5 | async-start | bytes 5242880 | tf_op jit(solution)/shard_map/all_to_all | solution.py:86
  269.1 63.9 %all-to-all-start.1 = ((bf16[16,40,2048]{2,1,0:T(8,128)(2,1)}), bf16[16,40,2048]{2,1,0:T(8,128)(2,1)}, u32[]{:S(2)}, u32[]{:S(2)}) async-start(bf16[16,40,2048]{2,1,0:T(8,128)(2,1)} %bitcast.112), calls=%async_computation.2 | async-start | bytes 5242880 | tf_op jit(solution)/shard_map/all_to_all | solution.py:79
  276.3 86.3 %all-reduce.3.cloned.1.call-start = ((), (), s32[]{:S(2)}) async-start(), calls=%async_computation.10 | async-start | bytes 2097152 | tf_op jit(solution)/shard_map/psum | solution.py:109
  339.9 26.5 %copy-start.1 = (bf16[1,2,2048,384]{3,2,1,0:T(8,128)(2,1)S(1)}, bf16[1,2,2048,384]{3,2,1,0:T(8,128)(2,1)}, u32[]{:S(2)}) copy-start(bf16[1,2,2048,384]{3,2,1,0:T(8,128)(2,1)} %param.10) | copy-start | bytes 9437188
Sparse Core Ops, SparseCore 0:
  88.5 18.4 all-gather.4
  161.6 16.0 all-gather.6
  191.4 14.3 reduce-scatter.4
  208.1 14.4 reduce-scatter.2
  340.1 22.5 all-reduce.2
where the time goes:
time: 374 us; the launch traced here: 373 us
  waiting for transfers between devices  183 us (49%)
  blocking collectives  70.3 us (19%)
  matrix products  55.3 us (15%)
  starting transfers between devices  21.1 us (6%)
  other arithmetic  18.9 us (5%)
  between operations  13.9 us (4%)
  local copies, waits for them, and re-layouts  10.1 us (3%)
    all_to_all x1, blocking collectives, shards(): lax.all_to_all(part_grad, 'expert', split_axis=0, concat_axis=0, tiled=True)  65.7 us
    all_to_all x1, waiting for transfers between devices, shards(): lax.all_to_all(part_rows, 'expert', split_axis=0, concat_axis=0, tiled=True)  54.1 us
    all_to_all x1, waiting for transfers between devices, shards(): lax.all_to_all(own_out.reshape(owners, share, features), 'expert', split_...  46.9 us
    all_to_all x1, waiting for transfers between devices, shards(): lax.all_to_all(own_grad.reshape(owners, share, features), 'expert', split...  46.5 us
    psum x1, waiting for transfers between devices, shards(): lax.psum(mixed_part.astype(jnp.bfloat16), 'hidden').astype(jnp.float32)  11.1 us
    reduce_scatter x1, waiting for transfers between devices, shards(): lax.psum_scatter(jnp.dot(piece, down_mat, preferred_element_type=jnp.floa...  10.3 us
    dot_general x1, matrix products, shards(): jnp.einsum('rd,jdf->jrf', x_rows, weights_gu, preferred_element_type=jnp....  8.72 us
    dot_general x1, matrix products, shards(): jnp.einsum('rd,fd->rf', d_rows, down_mat, preferred_element_type=jnp.floa...  7.52 us
  transfers between devices with their start and end apart: 8, of which 7 were waited for; matrix products, arithmetic and copies ran while one was open for 11% of the time, Pallas kernels for 0%

commit v1 on v0

v1 whole, which is shorter than its diff:
```python
import functools

import jax
import jax.numpy as jnp
from jax import lax
from jax.experimental import pallas as pl
from jax.experimental.pallas import tpu as pltpu
from jax.sharding import PartitionSpec as P

MESH = pl.DeviceIdType.MESH
PLANE = 4
F32 = jnp.float32
BF16 = jnp.bfloat16


def flip(a, k, size):
    out, bit = 0, 1
    while bit < size:
        digit = (a // bit) % 2
        out = out + bit * ((1 - digit) if (k // bit) % 2 else digit)
        bit *= 2
    return out


def place(planes):
    g, e, h = lax.axis_index("groups"), lax.axis_index("expert"), lax.axis_index("hidden")
    return g, e, h, e // PLANE, e % PLANE


def greet(n, g, e, h):
    barrier = pltpu.get_barrier_semaphore()

    def hello(i, _):
        to = (e + i) % n
        pl.semaphore_signal(barrier, inc=1, device_id=(g, to, h), device_id_type=MESH)
        pl.semaphore_signal(barrier, inc=1, device_id=(g, to, 1 - h), device_id_type=MESH)
        return 0

    lax.fori_loop(1, n, hello, 0)
    pl.semaphore_signal(barrier, inc=1, device_id=(g, e, 1 - h), device_id_type=MESH)
    pl.semaphore_wait(barrier, 2 * n - 1)


def gather_kernel(n, tok, cot, meta_in, gt, gc, meta, zs, zr, ps, pr, hs, hr, ms, mr, ls):
    planes = n // PLANE
    g, e, h, a, b = place(planes)
    near = [flip(b, 1, PLANE), flip(b, 2, PLANE)]
    ins, outs = (tok, cot), (gt, gc)
    greet(n, g, e, h)

    def rcopy(src, dst, s, r, to):
        return pltpu.make_async_remote_copy(
            src_ref=src, dst_ref=dst, send_sem=s, recv_sem=r, device_id=to, device_id_type=MESH
        )

    pending = []

    def go(copy):
        copy.start()
        pending.append(copy)
        return copy

    z = {}
    for k in range(1, planes):
        ak = flip(a, k, planes)
        for c in range(2):
            z[c, k] = go(rcopy(ins[c].at[h], outs[c].at[a, b, h], zs.at[c, k], zr.at[c, k],
                               (g, ak * PLANE + b, h)))

    def meta_copy(i):
        to = (e + i) % n
        return rcopy(meta_in.at[to], meta.at[e], ms.at[i], mr.at[i], (g, to, h))

    def send_meta(i, _):
        meta_copy(i).start()
        return 0

    def wait_meta(i, _):
        meta_copy(i).wait()
        return 0

    lax.fori_loop(1, n, send_meta, 0)
    local = [
        pltpu.make_async_copy(tok, gt.at[a, b], ls.at[0]),
        pltpu.make_async_copy(cot, gc.at[a, b], ls.at[1]),
        pltpu.make_async_copy(meta_in.at[e], meta.at[e], ls.at[2]),
    ]
    for copy in local:
        copy.start()

    hops, sib = {}, {}

    def hop(c, k, j, src, dst, to):
        hops[c, k, j] = go(rcopy(src, dst, ps.at[c, k, j], pr.at[c, k, j], to))

    def across(c, k, q, bq):
        ak = flip(a, k, planes)
        block = outs[c].at[ak, bq, h]
        sib[c, k, q] = go(rcopy(block, block, hs.at[c, k, q], hr.at[c, k, q], (g, e, 1 - h)))

    for k in range(planes + 2):
        if k < planes:
            ak = flip(a, k, planes)
            for c in range(2):
                first, second = near[c], near[1 - c]
                if k:
                    z[c, k].wait_recv()
                src = outs[c].at[ak, b, h] if k else ins[c].at[h]
                dst = outs[c].at[ak, b, h]
                hop(c, k, 0, src, dst, (g, a * PLANE + first, h))
                hop(c, k, 1, src, dst, (g, a * PLANE + second, h))
                if k:
                    across(c, k, 0, b)
        if 1 <= k <= planes:
            kk = k - 1
            ak = flip(a, kk, planes)
            for c in range(2):
                first, second = near[c], near[1 - c]
                hops[c, kk, 0].wait_recv()
                block = outs[c].at[ak, first, h]
                hop(c, kk, 2, block, block, (g, a * PLANE + second, h))
                across(c, kk, 1, first)
        if k >= 2:
            kk = k - 2
            for c in range(2):
                hops[c, kk, 1].wait_recv()
                across(c, kk, 2, near[1 - c])
                hops[c, kk, 2].wait_recv()
                across(c, kk, 3, flip(b, 3, PLANE))
    for copy in sib.values():
        copy.wait_recv()
    for copy in pending:
        copy.wait_send()
    lax.fori_loop(1, n, wait_meta, 0)
    for copy in local:
        copy.wait()


def gather(n, tok, cot, meta_in):
    planes = n // PLANE
    rows, width = tok.shape
    halves = (2, rows // 2, width)
    dma = pltpu.SemaphoreType.DMA
    anyspace = pl.BlockSpec(memory_space=pl.ANY)
    out = jax.ShapeDtypeStruct((planes, PLANE) + halves, BF16)
    return pl.pallas_call(
        functools.partial(gather_kernel, n),
        out_shape=(out, out, jax.ShapeDtypeStruct(meta_in.shape, F32)),
        in_specs=[anyspace] * 3,
        out_specs=(anyspace,) * 3,
        scratch_shapes=[
            dma((2, planes)), dma((2, planes)),
            dma((2, planes, 3)), dma((2, planes, 3)),
            dma((2, planes, 4)), dma((2, planes, 4)),
            dma((n,)), dma((n,)), dma((3,)),
        ],
        compiler_params=pltpu.CompilerParams(collective_id=0, has_side_effects=True),
        name="gather_rows",
    )(tok.reshape(halves), cot.reshape(halves), meta_in)


def reduce_kernel(n, pm, pg, route_in, om, og, route_out,
                  own, hbuf, nbuf, sbuf, zbuf, res,
                  os_, hs, hr, xs, xr, ys, yr, zs, zr, fs, fr, ms, mr, ls):
    planes = n // PLANE
    g, e, h, a, b = place(planes)
    near = [flip(b, 1, PLANE), flip(b, 2, PLANE)]
    opposite = flip(b, 3, PLANE)
    ins, outs = (pm, pg), (om, og)
    greet(n, g, e, h)

    def rcopy(src, dst, s, r, to):
        return pltpu.make_async_remote_copy(
            src_ref=src, dst_ref=dst, send_sem=s, recv_sem=r, device_id=to, device_id_type=MESH
        )

    pending = []

    def go(copy):
        copy.start()
        pending.append(copy)
        return copy

    def total(*parts):
        acc = parts[0].astype(F32)
        for part in parts[1:]:
            acc = acc + part.astype(F32)
        return acc.astype(BF16)

    order = list(range(1, planes)) + [0]
    load, sib = {}, {}
    for k in order:
        ak = flip(a, k, planes)
        for c in range(2):
            sib[c, k] = go(rcopy(ins[c].at[ak, :, 1 - h], hbuf.at[c, k], hs.at[c, k], hr.at[c, k],
                                 (g, e, 1 - h)))
            load[c, k] = pltpu.make_async_copy(ins[c].at[ak, :, h], own.at[c, k], os_.at[c, k])
            load[c, k].start()

    def route_copy(i, j):
        to = (e + i) % n
        return rcopy(route_in.at[to], route_out.at[e, h], ms.at[i, j], mr.at[i, j],
                     (g, to, (h + j) % 2))

    def send_route(i, _):
        route_copy(i, 0).start()
        route_copy(i, 1).start()
        return 0

    def wait_route(i, _):
        route_copy(i, 0).wait()
        route_copy(i, 1).wait()
        return 0

    route_copy(0, 1).start()
    lax.fori_loop(1, n, send_route, 0)
    mine = pltpu.make_async_copy(route_in.at[e], route_out.at[e, h], ls.at[0])
    mine.start()

    hop1, hop2, up = {}, {}, {}
    for step in range(planes + 2):
        if step < planes:
            k = order[step]
            for c in range(2):
                first, second = near[c], near[1 - c]
                load[c, k].wait()
                sib[c, k].wait_recv()
                for j, q in enumerate((opposite, first)):
                    own[c, k, q] = total(own[c, k, q], hbuf[c, k, q])
                    hop1[c, k, j] = go(rcopy(own.at[c, k, q], nbuf.at[c, k, j], xs.at[c, k, j],
                                             xr.at[c, k, j], (g, a * PLANE + first, h)))
                for q in (second, b):
                    own[c, k, q] = total(own[c, k, q], hbuf[c, k, q])
        if 1 <= step <= planes:
            k = order[step - 1]
            for c in range(2):
                second = near[1 - c]
                hop1[c, k, 0].wait_recv()
                own[c, k, second] = total(own[c, k, second], nbuf[c, k, 0])
                hop2[c, k] = go(rcopy(own.at[c, k, second], sbuf.at[c, k], ys.at[c, k],
                                      yr.at[c, k], (g, a * PLANE + second, h)))
                hop1[c, k, 1].wait_recv()
        if step >= 2:
            k = order[step - 2]
            for c in range(2):
                hop2[c, k].wait_recv()
                if k:
                    own[c, k, b] = total(own[c, k, b], nbuf[c, k, 1], sbuf[c, k])
                    ak = flip(a, k, planes)
                    up[c, k] = go(rcopy(own.at[c, k, b], zbuf.at[c, k], zs.at[c, k], zr.at[c, k],
                                        (g, ak * PLANE + b, h)))
    final = {}
    store = []
    for c in range(2):
        for k in range(1, planes):
            up[c, k].wait_recv()
        res[c] = total(own[c, 0, b], nbuf[c, 0, 1], sbuf[c, 0],
                       *[zbuf[c, k] for k in range(1, planes)])
        final[c] = go(rcopy(res.at[c], outs[c].at[h], fs.at[c], fr.at[c], (g, e, 1 - h)))
        copy = pltpu.make_async_copy(res.at[c], outs[c].at[h], ls.at[1 + c])
        copy.start()
        store.append(copy)
    for c in range(2):
        final[c].wait_recv()
        store[c].wait()
    for copy in pending:
        copy.wait_send()
    mine.wait()
    route_copy(0, 1).wait()
    lax.fori_loop(1, n, wait_route, 0)


def reduce_rows(n, part, mixed, grad, route, call_id):
    planes = n // PLANE
    width = mixed.shape[1]
    half = part // 2
    dma = pltpu.SemaphoreType.DMA
    anyspace = pl.BlockSpec(memory_space=pl.ANY)
    view = (planes, PLANE, 2, half, width)
    out = jax.ShapeDtypeStruct((2, half, width), BF16)
    vm = lambda *lead: pltpu.VMEM(lead + (half, width), BF16)
    om, og, ro = pl.pallas_call(
        functools.partial(reduce_kernel, n),
        out_shape=(out, out, jax.ShapeDtypeStruct((n, 2) + route.shape[1:], F32)),
        in_specs=[anyspace] * 3,
        out_specs=(anyspace,) * 3,
        scratch_shapes=[
            vm(2, planes, PLANE), vm(2, planes, PLANE), vm(2, planes, 2), vm(2, planes),
            vm(2, planes), vm(2),
            dma((2, planes)),
            dma((2, planes)), dma((2, planes)),
            dma((2, planes, 2)), dma((2, planes, 2)),
            dma((2, planes)), dma((2, planes)),
            dma((2, planes)), dma((2, planes)),
            dma((2,)), dma((2,)),
            dma((n, 2)), dma((n, 2)), dma((3,)),
        ],
        compiler_params=pltpu.CompilerParams(
            collective_id=call_id, has_side_effects=True, vmem_limit_bytes=48 * 2**20
        ),
        name="reduce_rows",
    )(mixed.reshape(view), grad.reshape(view), route)
    return om.reshape(part, width), og.reshape(part, width), ro


def shards(tokens, expert_ids, route_weights, cotangent, w_gate_up, w_down):
    part, features = tokens.shape
    n = lax.axis_size("expert")
    chosen = (expert_ids[:, :, None] == jnp.arange(n, dtype=jnp.int32)).astype(F32)
    dense = jnp.sum(chosen * route_weights[:, :, None], 1)
    meta_in = jnp.broadcast_to(dense.T[:, None, :], (n, 8, part))
    gt, gc, meta = gather(n, tokens, cotangent, meta_in)
    x_rows = gt.reshape(n * part, features)
    d_rows = gc.reshape(n * part, features)
    weight = meta[:, 0, :].reshape(n * part, 1)
    gate_w, up_w, down = w_gate_up[0, 0], w_gate_up[0, 1], w_down[0]
    gate = jnp.dot(x_rows, gate_w, preferred_element_type=F32)
    up = jnp.dot(x_rows, up_w, preferred_element_type=F32)
    grad_act = jnp.einsum("rd,fd->rf", d_rows, down, preferred_element_type=F32)
    sig = jax.nn.sigmoid(gate)
    act = gate * sig * up
    route = jnp.sum(act * grad_act, 1).reshape(n, 1, part)
    act_w = (act * weight).astype(BF16)
    grad_w = grad_act * weight
    grad_gate = (grad_w * up * sig * (1.0 + gate * (1.0 - sig))).astype(BF16)
    grad_up = (grad_w * gate * sig).astype(BF16)
    grad_down = jnp.einsum("rf,rd->fd", act_w, d_rows, preferred_element_type=F32).astype(BF16)
    route_in = jnp.broadcast_to(route, (n, 8, part))
    cuts = max(1, n // 16)
    step = features // cuts
    mixed, grad = [], []
    for i in range(cuts):
        cols = slice(i * step, (i + 1) * step)
        mixed_part = jnp.dot(act_w, down[:, cols], preferred_element_type=F32).astype(BF16)
        grad_part = (
            jnp.einsum("rf,df->rd", grad_gate, gate_w[cols], preferred_element_type=F32)
            + jnp.einsum("rf,df->rd", grad_up, up_w[cols], preferred_element_type=F32)
        ).astype(BF16)
        m, gr, ro = reduce_rows(n, part, mixed_part, grad_part, route_in, 1 + i)
        mixed.append(m)
        grad.append(gr)
        if i == 0:
            by_expert = ro[:, 0, 0] + ro[:, 1, 0]
        if i + 1 < cuts:
            m, gr, act_w, grad_gate, grad_up = lax.optimization_barrier(
                (m, gr, act_w, grad_gate, grad_up)
            )
    grad_route = jnp.sum(chosen * by_expert.T[:, None, :], 2)
    if cuts > 1:
        return (jnp.concatenate(mixed, 1), jnp.concatenate(grad, 1), grad_route, grad_down[None])
    return (mixed[0], grad[0], grad_route, grad_down[None])


def solution(mesh):
    rows = P(("groups", "expert"), None)
    return jax.shard_map(
        shards,
        mesh=mesh,
        in_specs=(rows, rows, rows, rows, P("expert", None, None, "hidden"), P("expert", "hidden", None)),
        out_specs=(rows, rows, rows, P(("groups", "expert"), "hidden", None)),
        check_vma=False,
    )
```

time: 374 us -> 256 us (0.68)
  Pallas kernels: 0 us -> 190 us
  waiting for transfers between devices: 183 us -> 0 us
  blocking collectives: 70.3 us -> 0 us
  starting transfers between devices: 21.1 us -> 0 us
  other arithmetic: 18.9 us -> 1.46 us
  between operations: 13.9 us -> 0.73 us
  local copies, waits for them, and re-layouts: 10.1 us -> 3.1 us
  matrix products: 55.3 us -> 60.5 us
    pallas_call x0 -> x2, Pallas kernels: none -> 190 us  [the longest x1 111 us: reduce_rows(): pl.pallas_call(functools.partial(reduce_kernel, n), out_shape=(out, out,...]
    all_to_all x3 -> x0, waiting for transfers between devices: 147 us -> none  [the longest x1 54.1 us: shards(): lax.all_to_all(part_rows, 'expert', split_axis=0, concat_axis=0, tiled=True)]
    all_to_all x1 -> x0, blocking collectives: 65.7 us -> none  [shards(): lax.all_to_all(part_grad, 'expert', split_axis=0, concat_axis=0, tiled=True)]
    all_to_all x3 -> x0, starting transfers between devices: 20.5 us -> none  [the longest x1 7.26 us: shards(): lax.all_to_all(own_out.reshape(owners, share, features), 'expert', split_...]
    reduce_scatter x2 -> x0, waiting for transfers between devices: 17.3 us -> none  [the longest x1 10.3 us: shards(): lax.psum_scatter(jnp.dot(piece, down_mat, preferred_element_type=jnp.floa...]
    psum x1 -> x0, waiting for transfers between devices: 11.1 us -> none  [shards(): lax.psum(mixed_part.astype(jnp.bfloat16), 'hidden').astype(jnp.float32)]
    all_gather x2 -> x0, waiting for transfers between devices: 7.24 us -> none  [the longest x1 7.22 us: shards(): lax.all_gather(got_grad[None], 'hidden', axis=0, tiled=True)]
    convert_element_type x4 -> x0, other arithmetic: 5.51 us -> none  [the longest x1 2.78 us: shards(): hidden_act = (gate_val * sigma * up_val).astype(jnp.bfloat16)]
  transfers between devices with their start and end apart: 8 -> 0, of which waited for: 7 -> 0; matrix products, arithmetic and copies ran while one was open for 11% -> 0% of each run, Pallas kernels for 0% -> 0%
where the time goes in v1:
time: 256 us; the launch traced here: 255 us
  Pallas kernels  190 us (74%)
  matrix products  60.5 us (24%)
  local copies, waits for them, and re-layouts  3.1 us (1%)
    pallas_call x1, Pallas kernels, reduce_rows(): pl.pallas_call(functools.partial(reduce_kernel, n), out_shape=(out, out,...  111 us
    pallas_call x1, Pallas kernels, gather(): pl.pallas_call(functools.partial(gather_kernel, n), out_shape=(out, out,...  79 us
    dot_general x1, matrix products, shards(): jnp.einsum('rf,df->rd', grad_up, up_w[cols], preferred_element_type=F32)  15.9 us
    dot_general x1, matrix products, shards(): jnp.einsum('rf,df->rd', grad_gate, gate_w[cols], preferred_element_type=F32)  9.38 us
    dot_general x1, matrix products, shards(): jnp.einsum('rf,rd->fd', act_w, d_rows, preferred_element_type=F32)  8.39 us
    dot_general x1, matrix products, shards(): up = jnp.dot(x_rows, up_w, preferred_element_type=F32)  7.08 us
    dot_general x1, matrix products, shards(): jnp.dot(act_w, down[:, cols], preferred_element_type=F32).astype(BF16)  6.93 us
    dot_general x1, matrix products, shards(): gate = jnp.dot(x_rows, gate_w, preferred_element_type=F32)  6.51 us

profile of v1, /device:TPU:9, one launch (start us, length us, event | category | flops | bytes accessed | tf_op | source)
XLA Modules:
  0.0 255.3 jit_solution(11854345896362597140)
XLA Ops:
  0.6 0.0 copy-start
  0.6 0.8 select_reduce_fusion.1
  1.5 0.6 broadcast_in_dim.8.meta_in
  2.1 79.0 %gather_rows.1 = (bf16[4,4,2,64,2048]{4,3,2,1,0:T(8,128)(2,1)}, bf16[4,4,2,64,2048]{4,3,2,1,0:T(8,128)(2,1)}, f32[16,8,128]{2,1,0:T(8,128)}) custom-call(bf16[2,64,2048]{2,1,0:T(8,128)(2,1)} %bitcast.41, bf16[2,64,2048]{2,1,0:T(8,128)(2,1)} %bitcast.42, f32[16,8,128]{2,1,0:T(8,128)} %broadcast_in_dim.8.meta_in), custom_call_target="tpu_custom_call" | custom-call | tf_op jit(solution)/shard_map/gather_rows/pallas_call | solution.py:146
  81.1 0.8 slice.17
  81.9 6.5 %fusion.9 = f32[2048,384]{0,1:T(8,128)S(1)} fusion(bf16[2048,2048]{1,0:T(8,128)(2,1)} %bitcast.52, bf16[1,2,2048,384]{3,2,1,0:T(8,128)(2,1)} %param.10), kind=kOutput, calls=%fused_computation.18 | convolution fusion | flops 3221225472 | bytes 13107200 | tf_op jit(solution)/shard_map/dot_general | solution.py:317
  88.5 0.0 copy-done.4
  88.5 0.0 copy-start.2
  88.5 7.1 %fusion.6 = f32[2048,384]{0,1:T(8,128)S(1)} fusion(bf16[2048,2048]{1,0:T(8,128)(2,1)} %bitcast.53, bf16[1,2,2048,384]{3,2,1,0:T(8,128)(2,1)S(1)} %copy-done.4), kind=kOutput, calls=%fused_computation.15 | convolution fusion | flops 3221225472 | bytes 13107200 | tf_op jit(solution)/shard_map/dot_general | solution.py:318
  95.6 8.4 %fusion = bf16[1,384,2048]{2,1,0:T(8,128)(2,1)} fusion(bf16[2048,2048]{1,0:T(8,128)(2,1)} %bitcast.50, f32[2048]{0:T(1024)S(1)} %bitcast.43, f32[2048,384]{0,1:T(8,128)S(1)} %fusion.6, f32[2048,384]{0,1:T(8,128)S(1)} %fusion.9), kind=kOutput, calls=%fused_computation.9 | convolution fusion | flops 3227516928 | bytes 16261120 | tf_op jit(solution)/shard_map/rf,rd->fd/dot_general | solution.py:327
  104.0 0.0 copy-done
  104.0 6.3 %multiply_reduce_fusion = (f32[2048]{0:T(1024)S(1)}, f32[2048,384]{0,1:T(8,128)S(1)}) fusion(f32[2048,384]{0,1:T(8,128)S(1)} %fusion.6, f32[2048,384]{0,1:T(8,128)S(1)} %fusion.9, bf16[2048,2048]{1,0:T(8,128)(2,1)} %bitcast.51, bf16[1,384,2048]{2,1,0:T(8,128)(2,1)S(1)} %copy-done), kind=kOutput, calls=%fused_computation.2 | convolution fusion | flops 3226728448 | bytes 19406848 | tf_op jit(solution)/shard_map/rd,fd->rf/dot_general | solution.py:319
  110.2 0.0 copy-start.3
  110.3 6.9 %convolution_convert_fusion = bf16[2048,2048]{1,0:T(8,128)(2,1)} fusion(bf16[1,384,2048]{2,1,0:T(8,128)(2,1)S(1)} %copy-done, f32[2048]{0:T(1024)S(1)} %bitcast.44, f32[2048,384]{0,1:T(8,128)S(1)} %fusion.6, f32[2048,384]{0,1:T(8,128)S(1)} %fusion.9), kind=kOutput, calls=%fused_computation.1 | convolution fusion | flops 3230924800 | bytes 16261120 | tf_op jit(solution)/shard_map/dot_general | solution.py:334
  117.2 0.0 copy-done.2
  117.2 0.0 copy-done.3
  117.2 9.4 %fusion.1 = f32[2048,2048]{1,0:T(8,128)} fusion(f32[2048,384]{0,1:T(8,128)S(1)} %fusion.9, f32[2048,384]{0,1:T(8,128)S(1)} %fusion.6, f32[2048,384]{0,1:T(8,128)S(1)} %get-tuple-element.17, f32[2048]{0:T(1024)S(1)} %bitcast.45, bf16[1,2,2048,384]{3,2,1,0:T(8,128)(2,1)S(1)} %copy-done.4), kind=kOutput, calls=%fused_computation.10 | convolution fusion | flops 3229876224 | bytes 27795456 | tf_op jit(solution)/shard_map/rf,df->rd/dot_general | solution.py:336
  126.6 15.9 %add_convert_fusion = bf16[2048,2048]{1,0:T(8,128)(2,1)} fusion(f32[2048,2048]{1,0:T(8,128)} %fusion.1, f32[2048,384]{0,1:T(8,128)} %copy-done.2, f32[2048,384]{0,1:T(8,128)} %copy-done.3, f32[2048]{0:T(1024)S(1)} %bitcast.46, bf16[1,2,2048,384]{3,2,1,0:T(8,128)(2,1)} %param.10), kind=kOutput, calls=%fused_computation | convolution fusion | flops 3235119104 | bytes 33038336 | tf_op jit(solution)/shard_map/rf,df->rd/dot_general | solution.py:337
  142.5 110.6 %reduce_rows.1 = (bf16[2,64,2048]{2,1,0:T(8,128)(2,1)S(1)}, bf16[2,64,2048]{2,1,0:T(8,128)(2,1)S(1)}, f32[16,2,8,128]{3,2,1,0:T(8,128)S(1)}) custom-call(bf16[4,4,2,64,2048]{4,3,2,1,0:T(8,128)(2,1)} %bitcast.40, bf16[4,4,2,64,2048]{4,3,2,1,0:T(8,128)(2,1)} %bitcast.39, f32[16,8,128]{2,1,0:T(8,128)S(1)} %broadcast_in_dim.10.route_in), custom_call_target="tpu_custom_call" | custom-call | tf_op jit(solution)/shard_map/reduce_rows/pallas_call | solution.py:282
  253.1 0.0 copy-done.5
  253.1 0.6 select_reduce_fusion
  253.7 0.8 copy.15
  254.5 0.8 copy.16
  255.3 0.0 copy-done.1
  (5 shorter events, 0.0 us)
Async XLA Ops:
  0.6 103.3 %copy-start = (bf16[1,384,2048]{2,1,0:T(8,128)(2,1)S(1)}, bf16[1,384,2048]{2,1,0:T(8,128)(2,1)}, u32[]{:S(2)}) copy-start(bf16[1,384,2048]{2,1,0:T(8,128)(2,1)} %param.11) | copy-start | bytes 4718596
  81.9 6.5 %copy-start.4 = (bf16[1,2,2048,384]{3,2,1,0:T(8,128)(2,1)S(1)}, bf16[1,2,2048,384]{3,2,1,0:T(8,128)(2,1)}, u32[]{:S(2)}) copy-start(bf16[1,2,2048,384]{3,2,1,0:T(8,128)(2,1)} %param.10) | copy-start | bytes 9437188
  88.5 28.7 %copy-start.2 = (f32[2048,384]{0,1:T(8,128)}, f32[2048,384]{0,1:T(8,128)S(1)}, u32[]{:S(2)}) copy-start(f32[2048,384]{0,1:T(8,128)S(1)} %fusion.9) | copy-start | bytes 9437188
  110.2 7.0 %copy-start.3 = (f32[2048,384]{0,1:T(8,128)}, f32[2048,384]{0,1:T(8,128)S(1)}, u32[]{:S(2)}) copy-start(f32[2048,384]{0,1:T(8,128)S(1)} %get-tuple-element.17) | copy-start | bytes 9437188
  142.5 110.6 %copy-start.5 = (s32[128,8]{0,1:T(8,128)S(1)}, s32[128,8]{0,1:T(8,128)}, u32[]{:S(2)}) copy-start(s32[128,8]{0,1:T(8,128)} %param.7) | copy-start | bytes 12292
  142.5 112.8 %copy-start.1 = (bf16[1,384,2048]{2,1,0:T(8,128)(2,1)S(1)}, bf16[1,384,2048]{2,1,0:T(8,128)(2,1)}, u32[]{:S(2)}) copy-start(bf16[1,384,2048]{2,1,0:T(8,128)(2,1)} %param.11) | copy-start | bytes 4718596

commit v2 on v1

--- a/solution.py
+++ b/solution.py
@@ -159,14 +159,14 @@
     )(tok.reshape(halves), cot.reshape(halves), meta_in)
 
 
-def reduce_kernel(n, pm, pg, route_in, om, og, route_out,
-                  own, hbuf, nbuf, sbuf, zbuf, res,
-                  os_, hs, hr, xs, xr, ys, yr, zs, zr, fs, fr, ms, mr, ls):
+def reduce_kernel(n, act_ref, gg_ref, gu_ref, down_ref, gw_ref, uw_ref, route_in, om, og, route_out,
+                  own, pbuf, hbuf, nbuf, sbuf, zbuf, res,
+                  hs, hr, xs, xr, ys, yr, zs, zr, fs, fr, ms, mr, ls):
     planes = n // PLANE
     g, e, h, a, b = place(planes)
     near = [flip(b, 1, PLANE), flip(b, 2, PLANE)]
     opposite = flip(b, 3, PLANE)
-    ins, outs = (pm, pg), (om, og)
+    outs = (om, og)
     greet(n, g, e, h)
 
     def rcopy(src, dst, s, r, to):
@@ -188,14 +188,32 @@
         return acc.astype(BF16)
 
     order = list(range(1, planes)) + [0]
-    load, sib = {}, {}
-    for k in order:
-        ak = flip(a, k, planes)
+    sib = {}
+    half = own.shape[3]
+    group = PLANE * 2 * half
+    tile = 256
+
+    def partial(k):
+        rows = pl.ds(pl.multiple_of(flip(a, k, planes) * group, group), group)
+        act, gg, gu = act_ref[rows, :], gg_ref[rows, :], gu_ref[rows, :]
+
+        def columns(t, _):
+            cols = pl.ds(pl.multiple_of(t * tile, tile), tile)
+            nt = (((1,), (1,)), ((), ()))
+            mixed = jnp.dot(act, down_ref[:, cols], preferred_element_type=F32)
+            grad = lax.dot_general(gg, gw_ref[cols, :], nt, preferred_element_type=F32)
+            grad = grad + lax.dot_general(gu, uw_ref[cols, :], nt, preferred_element_type=F32)
+            for c, term in enumerate((mixed, grad)):
+                term = term.astype(BF16).reshape(PLANE, 2, half, tile)
+                low, high = term[:, 0], term[:, 1]
+                own[c, k, :, :, cols] = jnp.where(h == 0, low, high)
+                pbuf[c, k, :, :, cols] = jnp.where(h == 0, high, low)
+            return 0
+
+        lax.fori_loop(0, own.shape[4] // tile, columns, 0)
         for c in range(2):
-            sib[c, k] = go(rcopy(ins[c].at[ak, :, 1 - h], hbuf.at[c, k], hs.at[c, k], hr.at[c, k],
+            sib[c, k] = go(rcopy(pbuf.at[c, k], hbuf.at[c, k], hs.at[c, k], hr.at[c, k],
                                  (g, e, 1 - h)))
-            load[c, k] = pltpu.make_async_copy(ins[c].at[ak, :, h], own.at[c, k], os_.at[c, k])
-            load[c, k].start()
 
     def route_copy(i, j):
         to = (e + i) % n
@@ -218,12 +236,14 @@
     mine.start()
 
     hop1, hop2, up = {}, {}, {}
+    partial(order[0])
     for step in range(planes + 2):
+        if step + 1 < planes:
+            partial(order[step + 1])
         if step < planes:
             k = order[step]
             for c in range(2):
                 first, second = near[c], near[1 - c]
-                load[c, k].wait()
                 sib[c, k].wait_recv()
                 for j, q in enumerate((opposite, first)):
                     own[c, k, q] = total(own[c, k, q], hbuf[c, k, q])
@@ -270,24 +290,23 @@
     lax.fori_loop(1, n, wait_route, 0)
 
 
-def reduce_rows(n, part, mixed, grad, route, call_id):
+def reduce_rows(n, part, act, gg, gu, down, gate_w, up_w, route, call_id):
     planes = n // PLANE
-    width = mixed.shape[1]
+    width = down.shape[1]
     half = part // 2
     dma = pltpu.SemaphoreType.DMA
     anyspace = pl.BlockSpec(memory_space=pl.ANY)
-    view = (planes, PLANE, 2, half, width)
+    inside = pl.BlockSpec(memory_space=pltpu.VMEM)
     out = jax.ShapeDtypeStruct((2, half, width), BF16)
     vm = lambda *lead: pltpu.VMEM(lead + (half, width), BF16)
     om, og, ro = pl.pallas_call(
         functools.partial(reduce_kernel, n),
         out_shape=(out, out, jax.ShapeDtypeStruct((n, 2) + route.shape[1:], F32)),
-        in_specs=[anyspace] * 3,
+        in_specs=[inside] * 6 + [anyspace],
         out_specs=(anyspace,) * 3,
         scratch_shapes=[
-            vm(2, planes, PLANE), vm(2, planes, PLANE), vm(2, planes, 2), vm(2, planes),
+            vm(2, planes, PLANE), vm(2, planes, PLANE), vm(2, planes, PLANE), vm(2, planes, 2), vm(2, planes),
             vm(2, planes), vm(2),
-            dma((2, planes)),
             dma((2, planes)), dma((2, planes)),
             dma((2, planes, 2)), dma((2, planes, 2)),
             dma((2, planes)), dma((2, planes)),
@@ -296,10 +315,10 @@
             dma((n, 2)), dma((n, 2)), dma((3,)),
         ],
         compiler_params=pltpu.CompilerParams(
-            collective_id=call_id, has_side_effects=True, vmem_limit_bytes=48 * 2**20
+            collective_id=call_id, has_side_effects=True, vmem_limit_bytes=60 * 2**20
         ),
         name="reduce_rows",
-    )(mixed.reshape(view), grad.reshape(view), route)
+    )(act, gg, gu, down, gate_w, up_w, route)
     return om.reshape(part, width), og.reshape(part, width), ro
 
 
@@ -331,12 +350,9 @@
     mixed, grad = [], []
     for i in range(cuts):
         cols = slice(i * step, (i + 1) * step)
-        mixed_part = jnp.dot(act_w, down[:, cols], preferred_element_type=F32).astype(BF16)
-        grad_part = (
-            jnp.einsum("rf,df->rd", grad_gate, gate_w[cols], preferred_element_type=F32)
-            + jnp.einsum("rf,df->rd", grad_up, up_w[cols], preferred_element_type=F32)
-        ).astype(BF16)
-        m, gr, ro = reduce_rows(n, part, mixed_part, grad_part, route_in, 1 + i)
+        m, gr, ro = reduce_rows(
+            n, part, act_w, grad_gate, grad_up, down[:, cols], gate_w[cols], up_w[cols], route_in, 1 + i
+        )
         mixed.append(m)
         grad.append(gr)
         if i == 0:

time: 256 us -> 237 us (0.926)
  matrix products: 60.5 us -> 28.8 us
  Pallas kernels: 190 us -> 199 us
  local copies, waits for them, and re-layouts: 3.1 us -> 5.79 us
    dot_general x3 -> x0, matrix products: 32.2 us -> none  [the longest x1 15.9 us: shards(): jnp.einsum('rf,df->rd', grad_up, up_w[cols], preferred_element_type=F32)]
    pallas_call x1, Pallas kernels: 111 us -> 120 us  [reduce_rows(): pl.pallas_call(functools.partial(reduce_kernel, n), out_shape=(out, out,...]
where the time goes in v2:
time: 237 us; the launch traced here: 236 us
  Pallas kernels  199 us (84%)
  matrix products  28.8 us (12%)
  local copies, waits for them, and re-layouts  5.79 us (2%)
    pallas_call x1, Pallas kernels, reduce_rows(): pl.pallas_call(functools.partial(reduce_kernel, n), out_shape=(out, out,...  120 us
    pallas_call x1, Pallas kernels, gather(): pl.pallas_call(functools.partial(gather_kernel, n), out_shape=(out, out,...  79 us
    dot_general x1, matrix products, shards(): gate = jnp.dot(x_rows, gate_w, preferred_element_type=F32)  8.22 us
    dot_general x1, matrix products, shards(): jnp.einsum('rf,rd->fd', act_w, d_rows, preferred_element_type=F32)  8.09 us
    dot_general x1, matrix products, shards(): grad_act = jnp.einsum('rd,fd->rf', d_rows, down, preferred_element_type=F32)  7.79 us

profile of v2, /device:TPU:9, one launch (start us, length us, event | category | flops | bytes accessed | tf_op | source)
XLA Modules:
  0.0 236.4 jit_solution(4624137612958194780)
XLA Ops:
  0.6 0.7 select_reduce_fusion.1
  1.4 0.6 broadcast_in_dim.8.meta_in
  2.0 79.0 %gather_rows.1 = (bf16[4,4,2,64,2048]{4,3,2,1,0:T(8,128)(2,1)}, bf16[4,4,2,64,2048]{4,3,2,1,0:T(8,128)(2,1)}, f32[16,8,128]{2,1,0:T(8,128)}) custom-call(bf16[2,64,2048]{2,1,0:T(8,128)(2,1)} %bitcast.31, bf16[2,64,2048]{2,1,0:T(8,128)(2,1)} %bitcast.32, f32[16,8,128]{2,1,0:T(8,128)} %broadcast_in_dim.8.meta_in), custom_call_target="tpu_custom_call" | custom-call | tf_op jit(solution)/shard_map/gather_rows/pallas_call | solution.py:146
  81.0 0.0 copy-start
  81.0 0.0 copy-start.6
  81.0 0.0 slice-start
  81.0 8.2 %fusion.3 = f32[2048,384]{1,0:T(8,128)S(1)} fusion(bf16[2048,2048]{1,0:T(8,128)(2,1)} %bitcast.43, bf16[1,2,2048,384]{3,2,1,0:T(8,128)(2,1)} %param.10), kind=kOutput, calls=%fused_computation.16 | convolution fusion | flops 3221225472 | bytes 13107200 | tf_op jit(solution)/shard_map/dot_general | solution.py:336
  89.2 0.0 copy-done
  89.2 0.0 copy-done.6
  89.2 0.0 copy-start.1
  89.3 0.0 slice-start.1
  89.3 4.7 %fusion.4 = f32[2048,384]{1,0:T(8,128)S(1)} fusion(bf16[2048,2048]{1,0:T(8,128)(2,1)S(1)} %bitcast.44, bf16[1,2,2048,384]{3,2,1,0:T(8,128)(2,1)S(1)} %copy-done), kind=kOutput, calls=%fused_computation.17 | convolution fusion | flops 3221225472 | bytes 13107200 | tf_op jit(solution)/shard_map/dot_general | solution.py:337
  93.9 0.8 slice.17
  94.8 0.0 slice-done
  94.8 7.8 %multiply_reduce_fusion = (f32[2048]{0:T(1024)S(1)}, bf16[2048,384]{1,0:T(8,128)(2,1)}, bf16[2048,384]{1,0:T(8,128)(2,1)}, bf16[2048,384]{1,0:T(8,128)(2,1)}) fusion(f32[2048,384]{1,0:T(8,128)S(1)} %fusion.4, f32[2048,384]{1,0:T(8,128)S(1)} %fusion.3, f32[2048]{0:T(1024)S(1)} %bitcast.38, bf16[2048,2048]{1,0:T(8,128)(2,1)S(1)} %bitcast.42, ...), kind=kOutput, calls=%fused_computation | convolution fusion | flops 3236952064 | bytes 20987904 | tf_op jit(solution)/shard_map/rd,fd->rf/dot_general | solution.py:338
  102.6 0.6 broadcast_in_dim.10.route_in
  103.2 2.0 slice_bitcast_fusion
  105.3 119.9 %reduce_rows.1 = (bf16[2,64,2048]{2,1,0:T(8,128)(2,1)}, bf16[2,64,2048]{2,1,0:T(8,128)(2,1)}, f32[16,2,8,128]{3,2,1,0:T(8,128)}) custom-call(bf16[2048,384]{1,0:T(8,128)(2,1)} %get-tuple-element.18.act_ref, bf16[2048,384]{1,0:T(8,128)(2,1)} %get-tuple-element.17.gg_ref, bf16[2048,384]{1,0:T(8,128)(2,1)} %get-tuple-element.19.gu_ref, ...), custom_call_target="tpu_custom_call" | custom-call | tf_op jit(solution)/shard_map/reduce_rows/pallas_call | solution.py:302
  225.2 0.9 slice_add_fusion
  226.1 0.6 select_reduce_fusion
  226.7 0.0 copy-done.2
  226.7 8.1 %fusion = bf16[1,384,2048]{2,1,0:T(8,128)(2,1)} fusion(bf16[2048,384]{1,0:T(8,128)(2,1)S(1)} %copy-done.2, bf16[2048,2048]{1,0:T(8,128)(2,1)} %bitcast.39), kind=kOutput, calls=%fused_computation.7 | convolution fusion | flops 3222011904 | bytes 11534336 | tf_op jit(solution)/shard_map/rf,rd->fd/dot_general | solution.py:346
  234.8 0.8 copy.34
  235.6 0.8 copy.35
  (10 shorter events, 0.0 us)
Async XLA Ops:
  81.0 8.3 %copy-start = (bf16[1,2,2048,384]{3,2,1,0:T(8,128)(2,1)S(1)}, bf16[1,2,2048,384]{3,2,1,0:T(8,128)(2,1)}, u32[]{:S(2)}) copy-start(bf16[1,2,2048,384]{3,2,1,0:T(8,128)(2,1)} %param.10) | copy-start | bytes 9437188
  81.0 8.3 %copy-start.6 = (bf16[4,4,2,64,2048]{4,3,2,1,0:T(8,128)(2,1)S(1)}, bf16[4,4,2,64,2048]{4,3,2,1,0:T(8,128)(2,1)}, u32[]{:S(2)}) copy-start(bf16[4,4,2,64,2048]{4,3,2,1,0:T(8,128)(2,1)} %get-tuple-element.10) | copy-start | bytes 25165828
  81.0 13.8 %slice-start = ((s8[8388608]{0:T(1024)(128)(4,1)}), s8[4194304]{0:T(1024)(128)(4,1)S(1)}, s32[]{:S(2)}) async-start(s8[8388608]{0:T(1024)(128)(4,1)} %bitcast.40), calls=%async_computation | async-start | bytes 8388608
  89.2 5.5 %copy-start.1 = (bf16[1,384,2048]{2,1,0:T(8,128)(2,1)S(1)}, bf16[1,384,2048]{2,1,0:T(8,128)(2,1)}, u32[]{:S(2)}) copy-start(bf16[1,384,2048]{2,1,0:T(8,128)(2,1)} %param.11) | copy-start | bytes 4718596
  89.3 5.5 %slice-start.1 = ((s8[8388608]{0:T(1024)(128)(4,1)}), s8[4194304]{0:T(1024)(128)(4,1)S(1)}, s32[]{:S(2)}) async-start(s8[8388608]{0:T(1024)(128)(4,1)} %bitcast.40), calls=%async_computation.1 | async-start | bytes 8388608
  105.3 120.8 %copy-start.5 = (s32[128,8]{0,1:T(8,128)S(1)}, s32[128,8]{0,1:T(8,128)}, u32[]{:S(2)}) copy-start(s32[128,8]{0,1:T(8,128)} %param.7) | copy-start | bytes 12292
  105.3 121.4 %copy-start.2 = (bf16[2048,384]{1,0:T(8,128)(2,1)S(1)}, bf16[2048,384]{1,0:T(8,128)(2,1)}, u32[]{:S(2)}) copy-start(bf16[2048,384]{1,0:T(8,128)(2,1)} %get-tuple-element.18.act_ref) | copy-start | bytes 4718596
  226.7 8.1 %copy-start.4 = (bf16[2,64,2048]{2,1,0:T(8,128)(2,1)S(1)}, bf16[2,64,2048]{2,1,0:T(8,128)(2,1)}, u32[]{:S(2)}) copy-start(bf16[2,64,2048]{2,1,0:T(8,128)(2,1)} %get-tuple-element.13) | copy-start | bytes 1572868
  226.7 8.9 %copy-start.3 = (bf16[2,64,2048]{2,1,0:T(8,128)(2,1)S(1)}, bf16[2,64,2048]{2,1,0:T(8,128)(2,1)}, u32[]{:S(2)}) copy-start(bf16[2,64,2048]{2,1,0:T(8,128)(2,1)} %get-tuple-element.14) | copy-start | bytes 1572868
